TPU v7x, 32 devices: a whole 2x2x4 slice. The times are simulated.
32 devices in a mesh: dp: 2 (over x), head: 1, row: 16 (over z, y, core).
Axes of the slice: x: 2, y: 2, z: 4, core: 2. Of those that a mesh axis runs over, the one named last changes fastest.
Arguments:
- pair_act: bfloat16 [256, 128, 128], P(('dp', 'row')), parts along dimension 0, may hold values from -12 to 12
- chain_id: int32 [256], P('dp'), parts along dimension 0, may hold values from 0 to 3, never falling along the last dimension, each value on 1 to 64 neighbouring positions
- residue_mask: int32 [256], P('dp'), parts along dimension 0, may hold values 0 or 1
- norm_gain: float32 [128], replicated, may hold values from 0.5 to 1.5
- w_proj: bfloat16 [128, 4, 128], P(None, 'head'), may hold values from -1.25 to 1.25
- w_bias: bfloat16 [128, 4], P(None, 'head'), may hold values from -0.9 to 0.9
- chain_bias: float32 [2, 4], P(None, 'head'), may hold values from -2 to 2
- w_out: bfloat16 [4, 32, 128], P('head'), may hold values from -0.5 to 0.5
- w_dist: bfloat16 [128, 64], replicated, may hold values from -0.5 to 0.5
- dist_bias: float32 [64], replicated, may hold values from -3 to 3
Outputs:
- new_pair: bfloat16 [256, 128, 128], P(('dp', 'row')), parts along dimension 0
- distogram: bfloat16 [256, 128, 64], P(('dp', 'row')), parts along dimension 0
There are 2 independent parts, one for each index of `dp`. A program takes and returns all parts, laid end to end along the dimension named above; an argument that names none is the same for every part. Nothing has to cross between parts.
Inputs may be any that keep to these rules, and one draw needn't show every extreme that they name: `chain_id`: chain ids never fall along the residues; no chain has more than half of the 128 residues.
All inputs are finite; a program needn't handle non-finite values.
Results may differ from a plain program's by a relative error of at most 0.013.
Values may be sent and summed in bfloat16 or wider, within the bound.
No kernel may reach another device: no remote copies, remote signals or barrier semaphores. Data moves between devices by JAX's collectives and lax.ppermute only.
A program may use at most 64 MiB of HBM per device.

v0:
```python
import functools

import jax
import jax.numpy as jnp
from jax import lax
from jax.experimental import pallas as pl
from jax.experimental.pallas import tpu as pltpu
from jax.sharding import PartitionSpec as P

LANES = 128
F32 = jnp.float32
BF16 = jnp.bfloat16


def dot_nt(a, b):
    return lax.dot_general(a, b, (((1,), (1,)), ((), ())), preferred_element_type=F32)


def dot_tn(a, b):
    return lax.dot_general(a, b, (((0,), (0,)), ((), ())), preferred_element_type=F32)


def dot_nn(a, b):
    return jnp.dot(a, b, preferred_element_type=F32)


def centring(chan):
    row = lax.broadcasted_iota(jnp.int32, (chan, chan), 0)
    col = lax.broadcasted_iota(jnp.int32, (chan, chan), 1)
    return (jnp.where(row == col, 1.0, 0.0) - 1.0 / chan).astype(BF16)


def layer_norm(values, centre, gain):
    centered = dot_nn(values, centre)
    variance = jnp.mean(centered * centered, -1, keepdims=True)
    return (centered * lax.rsqrt(variance + 1e-05) * gain).astype(BF16)


def swap_matrix(rows):
    size = 2 * rows * rows
    out = lax.broadcasted_iota(jnp.int32, (size, size), 0)
    col = lax.broadcasted_iota(jnp.int32, (size, size), 1)
    b, rest = out // (2 * rows), out % (2 * rows)
    wanted = (rest // rows) * (rows * rows) + (rest % rows) * rows + b
    return jnp.where(col == wanted, 1.0, 0.0).astype(BF16)


def pack_kernel(x_hbm, gain_hbm, wb_hbm, out_hbm, x_ref, gain_ref, wb_ref, out_ref, sems, out_sems):
    rows, n, chan = x_ref.shape
    peers = n // rows
    heads = wb_ref.shape[0]
    half = heads * rows // 2
    base = rows * rows
    fetch_gain = pltpu.make_async_copy(gain_hbm, gain_ref, sems.at[rows])
    fetch_wb = pltpu.make_async_copy(wb_hbm, wb_ref, sems.at[rows + 1])
    fetches = [pltpu.make_async_copy(x_hbm.at[k], x_ref.at[k], sems.at[k]) for k in range(rows)]
    for copy in (fetch_gain, fetch_wb, *fetches):
        copy.start()
    stores = []

    def store(first, count):
        at = pl.ds(first, count)
        copy = pltpu.make_async_copy(out_ref.at[:, at, :], out_hbm.at[:, at, :], out_sems.at[len(stores)])
        copy.start()
        stores.append(copy)

    centre = centring(chan)
    fetch_gain.wait()
    fetch_wb.wait()
    gain = gain_ref[...]
    wb = wb_ref[...].astype(F32)
    wb = jnp.concatenate([jnp.broadcast_to(wb[h : h + 1], (rows, chan)) for h in range(heads)], 0)
    owner = lax.broadcasted_iota(jnp.int32, wb.shape, 0) % rows
    bias = jnp.zeros((wb.shape[0], n), F32)
    for pair in range(rows // 2):
        both = []
        for k in (2 * pair, 2 * pair + 1):
            fetches[k].wait()
            x = x_ref[k]
            both.append(x.astype(F32).reshape(peers, rows, chan))
            mine = jnp.where(owner == k, wb, 0.0).astype(BF16)
            bias = bias + dot_nt(mine, layer_norm(x, centre, gain))
        out_ref[:, 2 * rows * pair : 2 * rows * (pair + 1), :] = jnp.concatenate(both, 1).astype(BF16)
        store(2 * rows * pair, 2 * rows)
    bias = bias.astype(BF16)
    for t in range(n // LANES):
        block = bias[:, t * LANES : (t + 1) * LANES]
        for d in range(peers):
            part = block[(d % 2) * half : (d % 2 + 1) * half]
            out_ref[d, base + t * half : base + (t + 1) * half] = part
    store(base, (n // LANES) * half)
    for copy in stores:
        copy.wait()


def prepare_kernel(
    heads,
    chain_ref, mask_ref, cb_ref, w_ref, db_ref, gain_ref, wo_ref, wd_ref,
    term_ref, wt_ref, dbc_ref, gain_out, wo_out, wd_out,
):
    gain_out[...] = gain_ref[...]
    wo_out[...] = wo_ref[...]
    wd_out[...] = wd_ref[...]
    n = chain_ref.shape[1]
    tiles = n // LANES
    chan = w_ref.shape[0]
    dim = w_ref.shape[2] // 4
    width = heads * dim

    def column_of(row):
        return jnp.transpose(jnp.broadcast_to(row, (LANES, LANES)))

    for kt in range(tiles):
        ks = slice(kt * LANES, (kt + 1) * LANES)
        chain_k = column_of(chain_ref[:, ks].astype(F32))
        mask_k = (column_of(mask_ref[:, ks].astype(F32)) - 1.0) * 1000000000.0
        for it in range(tiles):
            cs = slice(it * LANES, (it + 1) * LANES)
            same = chain_k == chain_ref[:, cs].astype(F32)
            for h in range(heads):
                term_ref[h, ks, cs] = jnp.where(same, cb_ref[1, h], cb_ref[0, h]) + mask_k
    for h in range(heads):
        turned = jnp.transpose(w_ref[:, h, :].astype(F32)).astype(BF16)
        for place, kind in enumerate((0, 2, 3, 1)):
            start = place * width + h * dim
            wt_ref[start : start + dim] = turned[kind * dim : (kind + 1) * dim]
    bins = dbc_ref.shape[0]
    db_rows = jnp.broadcast_to(jnp.concatenate([db_ref[...], db_ref[...]], 1)[:, :LANES], (LANES, LANES))
    dbc_ref[...] = jnp.transpose(db_rows)[:bins]


def project_kernel(heads, recv_ref, gain_ref, w_ref, x_s, spread_s, k_s, v_s, g_s, n_s):
    peers = recv_ref.shape[0]
    rows, n, chan = x_s.shape
    tiles = n // LANES
    dim = w_ref.shape[0] // (4 * heads)
    width = heads * dim
    base = rows * rows
    gain = gain_ref[...]
    swap = swap_matrix(rows)
    centre = centring(chan)
    group = 2 * rows

    for pair in range(peers // 2):
        at = slice(pair * group, (pair + 1) * group)
        both = jnp.concatenate([recv_ref[2 * pair, :base], recv_ref[2 * pair + 1, :base]], 0)
        x = dot_nn(swap, both).astype(BF16)
        x_s[:, at, :] = x.reshape(rows, group, chan)
        n_s[:, at, :] = layer_norm(x, centre, gain).reshape(rows, group, chan)

    w_qvg, w_k = w_ref[: 3 * width], w_ref[3 * width :]
    zero = jnp.zeros((dim, LANES), BF16)

    def project(j):
        normed = n_s[j]
        qvg = dot_nt(w_qvg, normed).astype(BF16)
        k_s[j] = dot_nt(normed, w_k).astype(BF16)
        v_s[j] = qvg[width : 2 * width]
        g_s[j] = jax.nn.sigmoid(qvg[2 * width :].astype(F32))
        for t in range(tiles):
            for h in range(heads):
                for other in range(heads):
                    block = qvg[h * dim : (h + 1) * dim, t * LANES : (t + 1) * LANES] if h == other else zero
                    spread_s[j, t, other * dim : (other + 1) * dim, h * LANES : (h + 1) * LANES] = block

    if tiles == 1:
        for j in range(rows):
            project(j)
    else:
        pl.loop(0, rows)(project)


def attend_kernel(
    heads, fused,
    recv_ref, other_ref, term_ref, wo_ref, wd_ref, db_ref, x_s, spread_s, k_s, v_s, g_s,
    out_ref, *refs,
):
    if fused:
        second_ref, bias_s = refs
    else:
        (bias_s,) = refs
    peers = recv_ref.shape[0]
    rows, n, chan = x_s.shape
    tiles = n // LANES
    dim = wo_ref.shape[0] // heads
    half = heads // 2
    base = rows * rows
    core = lax.axis_index("row") % 2

    for s in range(peers):
        at = slice(s * rows, (s + 1) * rows)
        for block, owner in ((recv_ref[s, base:], core), (other_ref[s], 1 - core)):
            extra = block.astype(F32)
            for t in range(tiles):
                cs = slice(t * LANES, (t + 1) * LANES)
                for h in range(half):
                    start = (t * half + h) * rows
                    head = owner * half + h
                    bias_s[head, at, cs] = extra[start : start + rows] + term_ref[head, at, cs]

    scaling = dim ** (-0.5)
    w_out = wo_ref[...]
    w_dist = wd_ref[...]
    d_bias = db_ref[:, :1]

    def score(j, t):
        return dot_nn(k_s[j], spread_s[j, t])

    def attend(j, t, scores):
        cs = slice(t * LANES, (t + 1) * LANES)
        gated = []
        for first in range(0, heads, 2):
            weights, scales = [], []
            for h in (first, first + 1):
                s = scores[:, h * LANES : (h + 1) * LANES] * scaling + bias_s[h, :, cs]
                e = jnp.exp(s - jnp.max(s, 0, keepdims=True))
                scales.append(1.0 / jnp.sum(e, 0, keepdims=True))
                weights.append(e.astype(BF16))
            o = dot_nn(v_s[j, first * dim : (first + 2) * dim, :], jnp.concatenate(weights, 1))
            for side in range(2):
                h = first + side
                part = o[side * dim : (side + 1) * dim, side * LANES : (side + 1) * LANES]
                gated.append((g_s[j, h * dim : (h + 1) * dim, cs] * (part * scales[side])).astype(BF16))
        return dot_tn(jnp.concatenate(gated, 0), w_out).astype(BF16)

    def residual(j, update):
        new = (x_s[j].astype(F32) + update.astype(F32)).astype(BF16)
        second_ref[j] = (dot_nt(w_dist, new) + d_bias).astype(BF16)
        return new.astype(F32).reshape(peers, rows, chan)

    if not fused:

        @pl.loop(0, rows)
        def _(j):
            for t in range(tiles):
                out_ref[j, t * LANES : (t + 1) * LANES] = attend(j, t, score(j, t))

        return

    both = []
    scores = score(0, 0)
    for j in range(rows):
        later = score(j + 1, 0) if j + 1 < rows and tiles == 1 else None
        updates = [attend(j, 0, scores)]
        for t in range(1, tiles):
            updates.append(attend(j, t, score(j, t)))
        both.append(residual(j, jnp.concatenate(updates, 0)))
        scores = later if tiles == 1 or j + 1 == rows else score(j + 1, 0)
        if j % 2:
            out_ref[:, (j - 1) * rows : (j + 1) * rows, :] = jnp.concatenate(both, 1).astype(BF16)
            both = []


def finish_kernel(recv_ref, mirror_ref, wd_ref, db_ref, new_hbm, dist_hbm, new_ref, dist_ref, sems):
    peers, _, chan = recv_ref.shape
    rows = new_ref.shape[0]
    group = 2 * rows
    swap = swap_matrix(rows)
    for pair in range(peers // 2):
        at = slice(pair * group, (pair + 1) * group)
        both = recv_ref[2 * pair : 2 * pair + 2].reshape(2 * rows * rows, chan)
        new_ref[:, at, :] = dot_nn(swap, both).astype(BF16).reshape(rows, group, chan)
    copies = [pltpu.make_async_copy(new_ref, new_hbm, sems.at[0])]
    copies[0].start()
    w_dist = wd_ref[...]
    d_bias = db_ref[:, :1]
    for i in range(rows):
        logits = (dot_nt(w_dist, new_ref[i]) + d_bias).astype(BF16)
        dist_ref[i] = (logits.astype(F32) + mirror_ref[i].astype(F32)).astype(BF16)
        if i % 2:
            at = pl.ds(i - 1, 2)
            copies.append(pltpu.make_async_copy(dist_ref.at[at], dist_hbm.at[at], sems.at[1 + i // 2]))
            copies[-1].start()
    for copy in copies:
        copy.wait()


def call(kernel, outs, args, scratch=(), smem=(), hbm=(), hbm_outs=False, limit=48):
    spaces = [pltpu.SMEM if i in smem else pl.ANY if i in hbm else pltpu.VMEM for i in range(len(args))]
    return pl.pallas_call(
        kernel,
        out_shape=[jax.ShapeDtypeStruct(s, d) for s, d in outs],
        in_specs=[pl.BlockSpec(memory_space=space) for space in spaces],
        out_specs=[pl.BlockSpec(memory_space=pl.ANY if hbm_outs else pltpu.VMEM)] * len(outs),
        scratch_shapes=list(scratch),
        compiler_params=pltpu.CompilerParams(vmem_limit_bytes=limit * 1024 * 1024),
    )(*args)


def swap_cores(values):
    peers = lax.axis_size("row")
    return lax.ppermute(values, "row", [(i, i ^ 1) for i in range(peers)])


def all_to_all(blocks):
    return lax.all_to_all(blocks, "row", split_axis=0, concat_axis=0, tiled=True)


def shards(
    pair_act, chain_id, residue_mask, norm_gain, w_proj, w_bias, chain_bias, w_out, w_dist, dist_bias,
):
    rows, n, chan = pair_act.shape
    peers = n // rows
    heads, dim = w_out.shape[0], w_out.shape[1]
    bins = w_dist.shape[1]
    tiles = n // LANES
    width = heads * dim
    fused = lax.axis_size("head") == 1
    gain = norm_gain[None, :]
    base = rows * rows
    length = base + tiles * heads * rows // 2

    (packed,) = call(
        pack_kernel,
        [((peers, length, chan), BF16)],
        [pair_act, gain, w_bias.T],
        scratch=[
            pltpu.VMEM(pair_act.shape, BF16),
            pltpu.VMEM(gain.shape, F32),
            pltpu.VMEM((heads, chan), BF16),
            pltpu.VMEM((peers, length, chan), BF16),
            pltpu.SemaphoreType.DMA((rows + 2,)),
            pltpu.SemaphoreType.DMA((rows // 2 + 1,)),
        ],
        hbm=(0, 1, 2),
        hbm_outs=True,
        limit=60,
    )
    received = all_to_all(packed)
    term, w_types, db_col, gain, w_out, wd_t = call(
        functools.partial(prepare_kernel, heads),
        [
            ((heads, n, n), F32), ((4 * width, chan), BF16), ((bins, LANES), F32),
            ((1, chan), F32), ((width, chan), BF16), ((bins, chan), BF16),
        ],
        [
            chain_id[None, :], residue_mask[None, :], chain_bias, w_proj, dist_bias[None, :],
            gain, w_out.reshape(width, chan), w_dist.T,
        ],
        smem=(2,),
    )
    other_bias = swap_cores(received[:, base:])
    x_cols, spread, keys, values, gates = call(
        functools.partial(project_kernel, heads),
        [
            ((rows, n, chan), BF16),
            ((rows, tiles, width, heads * LANES), BF16),
            ((rows, n, width), BF16),
            ((rows, width, n), BF16),
            ((rows, width, n), F32),
        ],
        [received, gain, w_types],
        scratch=[pltpu.VMEM((rows, n, chan), BF16)],
    )
    if fused:
        outs = [((peers, base, chan), BF16), ((rows, bins, n), BF16)]
    else:
        outs = [((rows, n, chan), BF16)]
    result = call(
        functools.partial(attend_kernel, heads, fused),
        outs,
        [received, other_bias, term, w_out, wd_t, db_col, x_cols, spread, keys, values, gates],
        scratch=[pltpu.VMEM((heads, n, n), F32)],
    )
    if fused:
        to_rows, mirror = result
    else:
        update = lax.psum(result[0], "head").astype(F32)
        new = (x_cols.astype(F32) + update).astype(BF16)
        logits = jnp.einsum("cb,jic->jbi", w_dist, new, preferred_element_type=F32)
        mirror = (logits + dist_bias[None, :, None]).astype(BF16)
        to_rows = new.reshape(rows, peers, rows, chan).transpose(1, 0, 2, 3).reshape(peers, base, chan)
    arrived = all_to_all(to_rows)
    new_rows, dist = call(
        finish_kernel,
        [((rows, n, chan), BF16), ((rows, bins, n), BF16)],
        [arrived, mirror, wd_t, db_col],
        scratch=[
            pltpu.VMEM((rows, n, chan), BF16),
            pltpu.VMEM((rows, bins, n), BF16),
            pltpu.SemaphoreType.DMA((1 + rows // 2,)),
        ],
        hbm_outs=True,
    )
    return new_rows, dist.transpose(0, 2, 1)


def solution(mesh):
    in_specs = (
        P(("dp", "row"), None, None),
        P("dp"),
        P("dp"),
        P(),
        P(None, "head", None),
        P(None, "head"),
        P(None, "head"),
        P("head", None, None),
        P(),
        P(),
    )
    out_specs = (P(("dp", "row"), None, None), P(("dp", "row"), None, None))
    return jax.shard_map(shards, mesh=mesh, in_specs=in_specs, out_specs=out_specs, check_vma=False)
```

profile of v0, /device:TPU:0, one launch (start us, length us, event | category | flops | bytes accessed | tf_op | source)
XLA Modules:
  0.0 42.7 jit_solution(3140082591819241329)
XLA Ops:
  0.6 3.8 %shard_map.113 = bf16[16,80,128]{2,1,0:T(8,128)(2,1)} custom-call(bf16[8,128,128]{2,1,0:T(8,128)(2,1)} %x_hbm.1, f32[1,128]{1,0:T(1,128)} %bitcast.10, bf16[4,128]{1,0:T(4,128)(2,1)} %bitcast.15), custom_call_target="tpu_custom_call" | custom-call | tf_op jit(solution)/shard_map/pallas_call | solution.py:280
  4.5 0.0 copy-start.1
  4.5 0.0 copy-start.2
  4.5 18.5 %all_to_all.10.recv_ref = bf16[16,80,128]{2,1,0:T(8,128)(2,1)S(1)} all-to-all(bf16[16,80,128]{2,1,0:T(8,128)(2,1)} %shard_map.113), channel_id=1, replica_groups=mesh['dp'=2,'head'=1,'row'=16] {'row'}, dimensions={0} | all-to-all | bytes 655360 | tf_op jit(solution)/shard_map/all_to_all | solution.py:296
  23.0 0.0 copy-start
  23.0 0.0 copy-start.5
  23.0 0.0 copy-start.6
  23.0 0.0 copy-start.7
  23.0 0.2 collective-permute-start
  23.2 0.0 copy-start.3
  23.2 0.0 copy-done.1
  23.2 0.0 copy-done.2
  23.2 0.7 %copy-done = bf16[128,4,128]{2,1,0:T(4,128)(2,1)S(1)} copy-done((bf16[128,4,128]{2,1,0:T(4,128)(2,1)S(1)}, bf16[128,4,128]{2,1,0:T(4,128)(2,1)}, u32[]{:S(2)}) %copy-start) | copy-done | bytes 131096
  23.9 0.0 copy-done.5
  23.9 0.0 copy-done.6
  23.9 0.0 copy-done.7
  23.9 0.0 copy-done.3
  23.9 0.0 copy-done.4
  23.9 0.8 %shard_map.114 = (f32[4,128,128]{2,1,0:T(8,128)S(1)}, bf16[512,128]{1,0:T(8,128)(2,1)S(1)}, f32[64,128]{1,0:T(8,128)S(1)}, f32[1,128]{1,0:T(1,128)S(1)}, bf16[12...) custom-call(s32[1,128]{1,0:T(1,128)S(1)} %bitcast.12, s32[1,128]{1,0:T(1,128)S(1)} %bitcast.13, f32[2,4]{1,0:T(2,128)S(1)} %copy-done.4, ...), custom_call_target="tpu_custom_call" | custom-call | tf_op jit(solution)/shard_map/pallas_call | solution.py:280
  24.7 1.1 %shard_map.115 = (bf16[8,128,128]{2,1,0:T(8,128)(2,1)S(1)}, bf16[8,1,128,512]{3,2,1,0:T(8,128)(2,1)S(1)}, bf16[8,128,128]{2,1,0:T(8,128)(2,1)S(1)}, bf16[8,128,128]{2,1,0:T(8,128)(2,1)S(1)}, f32[8,128,128]{2,1,0:T(8,128)S(1)}) custom-call(bf16[16,80,128]{2,1,0:T(8,128)(2,1)S(1)} %all_to_all.10.recv_ref, f32[1,128]{1,0:T(1,128)S(1)} %get-tuple-element.21.gain_ref, ...), custom_call_target="tpu_custom_call" | custom-call | tf_op jit(solution)/shard_map/pallas_call | solution.py:280
  25.8 0.0 collective-permute-done.other_ref
  25.8 2.5 %shard_map.116 = (bf16[16,64,128]{2,1,0:T(8,128)(2,1)S(1)}, bf16[8,64,128]{2,1,0:T(8,128)(2,1)S(1)}) custom-call(bf16[16,80,128]{2,1,0:T(8,128)(2,1)S(1)} %all_to_all.10.recv_ref, bf16[16,16,128]{2,1,0:T(8,128)(2,1)S(1)} %collective-permute-done.other_ref, f32[4,128,128]{2,1,0:T(8,128)S(1)} %get-tuple-element.17.term_ref, ...), custom_call_target="tpu_custom_call" | custom-call | tf_op jit(solution)/shard_map/pallas_call | solution.py:280
  28.4 13.2 %all_to_all.11.recv_ref = bf16[16,64,128]{2,1,0:T(8,128)(2,1)S(1)} all-to-all(bf16[16,64,128]{2,1,0:T(8,128)(2,1)S(1)} %get-tuple-element.28), channel_id=1, replica_groups=mesh['dp'=2,'head'=1,'row'=16] {'row'}, dimensions={0} | all-to-all | bytes 524288 | tf_op jit(solution)/shard_map/all_to_all | solution.py:296
  41.6 1.1 %shard_map.117 = (bf16[8,128,128]{2,1,0:T(8,128)(2,1)}, bf16[8,64,128]{2,1,0:T(8,128)(2,1)}) custom-call(bf16[16,64,128]{2,1,0:T(8,128)(2,1)S(1)} %all_to_all.11.recv_ref, bf16[8,64,128]{2,1,0:T(8,128)(2,1)S(1)} %get-tuple-element.29.mirror_ref, bf16[64,128]{1,0:T(8,128)(2,1)S(1)} %get-tuple-element.19.wd_ref, f32[64,128]{1,0:T(8,128)S(1)} %get-tuple-element.20.db_ref), custom_call_target="tpu_custom_call" | custom-call | tf_op jit(solution)/shard_map/pallas_call | solution.py:280
  (2 shorter events, 0.0 us)
Async XLA Ops:
  4.5 18.7 %copy-start.1 = (bf16[4,32,128]{2,1,0:T(8,128)(2,1)S(1)}, bf16[4,32,128]{2,1,0:T(8,128)(2,1)}, u32[]{:S(2)}) copy-start(bf16[4,32,128]{2,1,0:T(8,128)(2,1)} %param.17) | copy-start | bytes 98308
  4.5 18.7 %copy-start.2 = (bf16[128,64]{0,1:T(8,128)(2,1)S(1)}, bf16[128,64]{0,1:T(8,128)(2,1)}, u32[]{:S(2)}) copy-start(bf16[128,64]{0,1:T(8,128)(2,1)} %param.18) | copy-start | bytes 49156
  23.0 0.9 %copy-start = (bf16[128,4,128]{2,1,0:T(4,128)(2,1)S(1)}, bf16[128,4,128]{2,1,0:T(4,128)(2,1)}, u32[]{:S(2)}) copy-start(bf16[128,4,128]{2,1,0:T(4,128)(2,1)} %w_ref.1) | copy-start | bytes 393220
  23.0 0.9 %copy-start.5 = (s32[128]{0:T(128)S(1)}, s32[128]{0:T(128)}, u32[]{:S(2)}) copy-start(s32[128]{0:T(128)} %param.11) | copy-start | bytes 1540
  23.0 0.9 %copy-start.6 = (s32[128]{0:T(128)S(1)}, s32[128]{0:T(128)}, u32[]{:S(2)}) copy-start(s32[128]{0:T(128)} %param.12) | copy-start | bytes 1540
  23.0 0.9 %copy-start.7 = (f32[64]{0:T(128)S(1)}, f32[64]{0:T(128)}, u32[]{:S(2)}) copy-start(f32[64]{0:T(128)} %param.19) | copy-start | bytes 772
  23.0 2.8 %collective-permute-start = (bf16[16,16,128]{2,1,0:T(8,128)(2,1)S(1)}, bf16[16,16,128]{2,1,0:T(8,128)(2,1)S(1)}, u32[]{:S(2)}, u32[]{:S(2)}) collective-permute-start(bf16[16,16,128]{2,1,0:T(8,128)(2,1)S(1)} %slice.4), channel_id=1, source_target_pairs={{0,1},{1,0},{2,3},{3,2},{4,5},{5,4},{6,7},{7,6},{8,9},{9,8},{10,11... | collective-permute-start | bytes 196616 | tf_op jit(solution)/shard_map/ppermute | solution.py:292
  23.2 0.7 %copy-start.3 = (f32[128]{0:T(128)S(1)}, f32[128]{0:T(128)}, u32[]{:S(2)}) copy-start(f32[128]{0:T(128)} %param.13) | copy-start | bytes 1540
  23.2 0.7 %copy-start.4 = (f32[2,4]{1,0:T(2,128)S(1)}, f32[2,4]{1,0:T(2,128)}, u32[]{:S(2)}) copy-start(f32[2,4]{1,0:T(2,128)} %cb_ref.1) | copy-start | bytes 100
where the time goes:
time: 43.1 us; the launch traced here: 42.7 us
  blocking collectives  31.7 us (74%)
  Pallas kernels  9.4 us (22%)
  local copies, waits for them, and re-layouts  0.73 us (2%)
  between operations  0.7 us (2%)
    all_to_all x2, blocking collectives, all_to_all(): lax.all_to_all(blocks, 'row', split_axis=0, concat_axis=0, tiled=True)  31.7 us
    pallas_call x5, Pallas kernels, call(): pl.pallas_call(kernel, out_shape=[jax.ShapeDtypeStruct(s, d) for s, d in...  9.4 us
  transfers between devices with their start and end apart: 1, of which 0 were waited for; matrix products, arithmetic and copies ran while one was open for 0% of the time, Pallas kernels for 4%

commit v1 on v0

--- a/solution.py
+++ b/solution.py
@@ -64,24 +64,21 @@
         copy.start()
         stores.append(copy)
 
+    for copy in (fetch_gain, fetch_wb, *fetches):
+        copy.wait()
+    for pair in range(rows // 2):
+        both = [x_ref[k].astype(F32).reshape(peers, rows, chan) for k in (2 * pair, 2 * pair + 1)]
+        out_ref[:, 2 * rows * pair : 2 * rows * (pair + 1), :] = jnp.concatenate(both, 1).astype(BF16)
+    store(0, base)
     centre = centring(chan)
-    fetch_gain.wait()
-    fetch_wb.wait()
     gain = gain_ref[...]
     wb = wb_ref[...].astype(F32)
     wb = jnp.concatenate([jnp.broadcast_to(wb[h : h + 1], (rows, chan)) for h in range(heads)], 0)
     owner = lax.broadcasted_iota(jnp.int32, wb.shape, 0) % rows
     bias = jnp.zeros((wb.shape[0], n), F32)
-    for pair in range(rows // 2):
-        both = []
-        for k in (2 * pair, 2 * pair + 1):
-            fetches[k].wait()
-            x = x_ref[k]
-            both.append(x.astype(F32).reshape(peers, rows, chan))
-            mine = jnp.where(owner == k, wb, 0.0).astype(BF16)
-            bias = bias + dot_nt(mine, layer_norm(x, centre, gain))
-        out_ref[:, 2 * rows * pair : 2 * rows * (pair + 1), :] = jnp.concatenate(both, 1).astype(BF16)
-        store(2 * rows * pair, 2 * rows)
+    for k in range(rows):
+        mine = jnp.where(owner == k, wb, 0.0).astype(BF16)
+        bias = bias + dot_nt(mine, layer_norm(x_ref[k], centre, gain))
     bias = bias.astype(BF16)
     for t in range(n // LANES):
         block = bias[:, t * LANES : (t + 1) * LANES]
@@ -320,7 +317,7 @@
             pltpu.VMEM((heads, chan), BF16),
             pltpu.VMEM((peers, length, chan), BF16),
             pltpu.SemaphoreType.DMA((rows + 2,)),
-            pltpu.SemaphoreType.DMA((rows // 2 + 1,)),
+            pltpu.SemaphoreType.DMA((2,)),
         ],
         hbm=(0, 1, 2),
         hbm_outs=True,
@@ -338,6 +335,9 @@
             gain, w_out.reshape(width, chan), w_dist.T,
         ],
         smem=(2,),
+    )
+    received, term, w_types, db_col, gain, w_out, wd_t = lax.optimization_barrier(
+        (received, term, w_types, db_col, gain, w_out, wd_t)
     )
     other_bias = swap_cores(received[:, base:])
     x_cols, spread, keys, values, gates = call(

time: 43.1 us -> 40.3 us (0.935)
  blocking collectives: 31.7 us -> 13.2 us
  waiting for transfers between devices: 0.01 us -> 9.63 us
  starting transfers between devices: 0.18 us -> 7.64 us
  Pallas kernels: 9.4 us -> 8.07 us
    all_to_all x2 -> x1, blocking collectives: 31.7 us -> 13.2 us  [all_to_all(): lax.all_to_all(blocks, 'row', split_axis=0, concat_axis=0, tiled=True)]
    all_to_all x0 -> x1, waiting for transfers between devices: none -> 9.57 us  [all_to_all(): lax.all_to_all(blocks, 'row', split_axis=0, concat_axis=0, tiled=True)]
    all_to_all x0 -> x1, starting transfers between devices: none -> 7.53 us  [all_to_all(): lax.all_to_all(blocks, 'row', split_axis=0, concat_axis=0, tiled=True)]
    pallas_call x5, Pallas kernels: 9.4 us -> 8.07 us  [call(): pl.pallas_call(kernel, out_shape=[jax.ShapeDtypeStruct(s, d) for s, d in...]
  transfers between devices with their start and end apart: 1 -> 2, of which waited for: 0 -> 2; matrix products, arithmetic and copies ran while one was open for 0% -> 0% of each run, Pallas kernels for 4% -> 5%
where the time goes in v1:
time: 40.3 us; the launch traced here: 40 us
  blocking collectives  13.2 us (33%)
  waiting for transfers between devices  9.63 us (24%)
  Pallas kernels  8.07 us (20%)
  starting transfers between devices  7.64 us (19%)
  between operations  0.77 us (2%)
  local copies, waits for them, and re-layouts  0.66 us (2%)
    all_to_all x1, blocking collectives, all_to_all(): lax.all_to_all(blocks, 'row', split_axis=0, concat_axis=0, tiled=True)  13.2 us
    all_to_all x1, waiting for transfers between devices, all_to_all(): lax.all_to_all(blocks, 'row', split_axis=0, concat_axis=0, tiled=True)  9.57 us
    pallas_call x5, Pallas kernels, call(): pl.pallas_call(kernel, out_shape=[jax.ShapeDtypeStruct(s, d) for s, d in...  8.07 us
    all_to_all x1, starting transfers between devices, all_to_all(): lax.all_to_all(blocks, 'row', split_axis=0, concat_axis=0, tiled=True)  7.53 us
  transfers between devices with their start and end apart: 2, of which 2 were waited for; matrix products, arithmetic and copies ran while one was open for 0% of the time, Pallas kernels for 5%

profile of v1, /device:TPU:0, one launch (start us, length us, event | category | flops | bytes accessed | tf_op | source)
XLA Modules:
  0.0 40.0 jit_solution(4006958998868653703)
XLA Ops:
  0.6 2.5 %shard_map.113 = bf16[16,80,128]{2,1,0:T(8,128)(2,1)} custom-call(bf16[8,128,128]{2,1,0:T(8,128)(2,1)} %x_hbm.1, f32[1,128]{1,0:T(1,128)} %bitcast.10, bf16[4,128]{1,0:T(4,128)(2,1)} %bitcast.15), custom_call_target="tpu_custom_call" | custom-call | tf_op jit(solution)/shard_map/pallas_call | solution.py:277
  3.1 0.0 copy-start
  3.1 0.0 copy-start.1
  3.2 0.0 copy-start.2
  3.2 0.0 copy-start.5
  3.2 0.0 copy-start.6
  3.2 0.0 copy-start.7
  3.2 7.5 %all-to-all-start = ((bf16[16,80,128]{2,1,0:T(8,128)(2,1)}), bf16[16,80,128]{2,1,0:T(8,128)(2,1)S(1)}, u32[]{:S(2)}, u32[]{:S(2)}) async-start(bf16[16,80,128]{2,1,0:T(8,128)(2,1)} %shard_map.113), calls=%async_computation | async-start | bytes 655360 | tf_op jit(solution)/shard_map/all_to_all | solution.py:293
  10.7 0.0 copy-start.3
  10.8 0.0 copy-start.4
  10.8 0.0 copy-done
  10.8 0.0 copy-done.1
  10.8 0.0 copy-done.2
  10.8 0.0 copy-done.5
  10.8 0.6 %copy-done.3 = f32[128]{0:T(128)S(1)} copy-done((f32[128]{0:T(128)S(1)}, f32[128]{0:T(128)}, u32[]{:S(2)}) %copy-start.3) | copy-done | bytes 536
  11.4 0.0 copy-done.4
  11.4 0.8 %shard_map.114 = (f32[4,128,128]{2,1,0:T(8,128)S(1)}, bf16[512,128]{1,0:T(8,128)(2,1)S(1)}, f32[64,128]{1,0:T(8,128)S(1)}, f32[1,128]{1,0:T(1,128)S(1)}, bf16[12...) custom-call(s32[1,128]{1,0:T(1,128)S(1)} %bitcast.12, s32[1,128]{1,0:T(1,128)S(1)} %bitcast.13, f32[2,4]{1,0:T(2,128)S(1)} %copy-done.4, ...), custom_call_target="tpu_custom_call" | custom-call | tf_op jit(solution)/shard_map/pallas_call | solution.py:277
  12.3 9.6 %all-to-all-done.recv_ref = bf16[16,80,128]{2,1,0:T(8,128)(2,1)S(1)} async-done(((bf16[16,80,128]{2,1,0:T(8,128)(2,1)}), bf16[16,80,128]{2,1,0:T(8,128)(2,1)S(1)}, u32[]{:S(2)}, u32[]{:S(2)}) %all-to-all-start) | async-done | bytes 327712 | tf_op jit(solution)/shard_map/all_to_all | solution.py:293
  21.8 0.1 collective-permute-start
  22.0 1.1 %shard_map.115 = (bf16[8,128,128]{2,1,0:T(8,128)(2,1)S(1)}, bf16[8,1,128,512]{3,2,1,0:T(8,128)(2,1)S(1)}, bf16[8,128,128]{2,1,0:T(8,128)(2,1)S(1)}, bf16[8,128,128]{2,1,0:T(8,128)(2,1)S(1)}, f32[8,128,128]{2,1,0:T(8,128)S(1)}) custom-call(bf16[16,80,128]{2,1,0:T(8,128)(2,1)S(1)} %all-to-all-done.recv_ref, f32[1,128]{1,0:T(1,128)S(1)} %get-tuple-element.35.gain_ref, ...), custom_call_target="tpu_custom_call" | custom-call | tf_op jit(solution)/shard_map/pallas_call | solution.py:277
  23.0 0.1 collective-permute-done.other_ref
  23.1 2.5 %shard_map.116 = (bf16[16,64,128]{2,1,0:T(8,128)(2,1)S(1)}, bf16[8,64,128]{2,1,0:T(8,128)(2,1)S(1)}) custom-call(bf16[16,80,128]{2,1,0:T(8,128)(2,1)S(1)} %all-to-all-done.recv_ref, bf16[16,16,128]{2,1,0:T(8,128)(2,1)S(1)} %collective-permute-done.other_ref, f32[4,128,128]{2,1,0:T(8,128)S(1)} %get-tuple-element.31.term_ref, ...), custom_call_target="tpu_custom_call" | custom-call | tf_op jit(solution)/shard_map/pallas_call | solution.py:277
  25.6 13.2 %all_to_all.10.recv_ref = bf16[16,64,128]{2,1,0:T(8,128)(2,1)S(1)} all-to-all(bf16[16,64,128]{2,1,0:T(8,128)(2,1)S(1)} %get-tuple-element.42), channel_id=1, replica_groups=mesh['dp'=2,'head'=1,'row'=16] {'row'}, dimensions={0} | all-to-all | bytes 524288 | tf_op jit(solution)/shard_map/all_to_all | solution.py:293
  38.8 1.1 %shard_map.117 = (bf16[8,128,128]{2,1,0:T(8,128)(2,1)}, bf16[8,64,128]{2,1,0:T(8,128)(2,1)}) custom-call(bf16[16,64,128]{2,1,0:T(8,128)(2,1)S(1)} %all_to_all.10.recv_ref, bf16[8,64,128]{2,1,0:T(8,128)(2,1)S(1)} %get-tuple-element.43.mirror_ref, bf16[64,128]{1,0:T(8,128)(2,1)S(1)} %get-tuple-element.33.wd_ref, f32[64,128]{1,0:T(8,128)S(1)} %get-tuple-element.34.db_ref), custom_call_target="tpu_custom_call" | custom-call | tf_op jit(solution)/shard_map/pallas_call | solution.py:277
  (3 shorter events, 0.0 us)
Async XLA Ops:
  3.1 7.6 %copy-start = (bf16[128,4,128]{2,1,0:T(4,128)(2,1)S(1)}, bf16[128,4,128]{2,1,0:T(4,128)(2,1)}, u32[]{:S(2)}) copy-start(bf16[128,4,128]{2,1,0:T(4,128)(2,1)} %w_ref.1) | copy-start | bytes 393220
  3.1 7.6 %copy-start.1 = (bf16[4,32,128]{2,1,0:T(8,128)(2,1)S(1)}, bf16[4,32,128]{2,1,0:T(8,128)(2,1)}, u32[]{:S(2)}) copy-start(bf16[4,32,128]{2,1,0:T(8,128)(2,1)} %param.17) | copy-start | bytes 98308
  3.2 7.6 %copy-start.2 = (bf16[128,64]{0,1:T(8,128)(2,1)S(1)}, bf16[128,64]{0,1:T(8,128)(2,1)}, u32[]{:S(2)}) copy-start(bf16[128,64]{0,1:T(8,128)(2,1)} %param.18) | copy-start | bytes 49156
  3.2 7.6 %copy-start.5 = (s32[128]{0:T(128)S(1)}, s32[128]{0:T(128)}, u32[]{:S(2)}) copy-start(s32[128]{0:T(128)} %param.11) | copy-start | bytes 1540
  3.2 7.6 %copy-start.6 = (s32[128]{0:T(128)S(1)}, s32[128]{0:T(128)}, u32[]{:S(2)}) copy-start(s32[128]{0:T(128)} %param.12) | copy-start | bytes 1540
  3.2 7.6 %copy-start.7 = (f32[64]{0:T(128)S(1)}, f32[64]{0:T(128)}, u32[]{:S(2)}) copy-start(f32[64]{0:T(128)} %param.19) | copy-start | bytes 772
  3.2 18.6 %all-to-all-start = ((bf16[16,80,128]{2,1,0:T(8,128)(2,1)}), bf16[16,80,128]{2,1,0:T(8,128)(2,1)S(1)}, u32[]{:S(2)}, u32[]{:S(2)}) async-start(bf16[16,80,128]{2,1,0:T(8,128)(2,1)} %shard_map.113), calls=%async_computation | async-start | bytes 655360 | tf_op jit(solution)/shard_map/all_to_all | solution.py:293
  10.7 0.7 %copy-start.3 = (f32[128]{0:T(128)S(1)}, f32[128]{0:T(128)}, u32[]{:S(2)}) copy-start(f32[128]{0:T(128)} %param.13) | copy-start | bytes 1540
  10.8 0.7 %copy-start.4 = (f32[2,4]{1,0:T(2,128)S(1)}, f32[2,4]{1,0:T(2,128)}, u32[]{:S(2)}) copy-start(f32[2,4]{1,0:T(2,128)} %cb_ref.1) | copy-start | bytes 100
  21.8 1.3 %collective-permute-start = (bf16[16,16,128]{2,1,0:T(8,128)(2,1)S(1)}, bf16[16,16,128]{2,1,0:T(8,128)(2,1)S(1)}, u32[]{:S(2)}, u32[]{:S(2)}) collective-permute-start(bf16[16,16,128]{2,1,0:T(8,128)(2,1)S(1)} %slice.3), channel_id=1, source_target_pairs={{0,1},{1,0},{2,3},{3,2},{4,5},{5,4},{6,7},{7,6},{8,9},{9,8},{10,11... | collective-permute-start | bytes 196616 | tf_op jit(solution)/shard_map/ppermute | solution.py:289

commit v2 on v1

--- a/solution.py
+++ b/solution.py
@@ -10,6 +10,7 @@
 LANES = 128
 F32 = jnp.float32
 BF16 = jnp.bfloat16
+LOG2E = 1.4426950408889634
 
 
 def dot_nt(a, b):
@@ -45,7 +46,7 @@
     return jnp.where(col == wanted, 1.0, 0.0).astype(BF16)
 
 
-def pack_kernel(x_hbm, gain_hbm, wb_hbm, out_hbm, x_ref, gain_ref, wb_ref, out_ref, sems, out_sems):
+def pack_kernel(x_hbm, gain_hbm, wb_hbm, out_hbm, x_ref, gain_ref, wb_ref, n_ref, out_ref, sems, out_sems):
     rows, n, chan = x_ref.shape
     peers = n // rows
     heads = wb_ref.shape[0]
@@ -77,8 +78,10 @@
     owner = lax.broadcasted_iota(jnp.int32, wb.shape, 0) % rows
     bias = jnp.zeros((wb.shape[0], n), F32)
     for k in range(rows):
+        n_ref[k] = layer_norm(x_ref[k], centre, gain)
+    for k in range(rows):
         mine = jnp.where(owner == k, wb, 0.0).astype(BF16)
-        bias = bias + dot_nt(mine, layer_norm(x_ref[k], centre, gain))
+        bias = bias + dot_nt(mine, n_ref[k])
     bias = bias.astype(BF16)
     for t in range(n // LANES):
         block = bias[:, t * LANES : (t + 1) * LANES]
@@ -115,7 +118,7 @@
             cs = slice(it * LANES, (it + 1) * LANES)
             same = chain_k == chain_ref[:, cs].astype(F32)
             for h in range(heads):
-                term_ref[h, ks, cs] = jnp.where(same, cb_ref[1, h], cb_ref[0, h]) + mask_k
+                term_ref[h, ks, cs] = (jnp.where(same, cb_ref[1, h], cb_ref[0, h]) + mask_k) * LOG2E
     for h in range(heads):
         turned = jnp.transpose(w_ref[:, h, :].astype(F32)).astype(BF16)
         for place, kind in enumerate((0, 2, 3, 1)):
@@ -173,9 +176,9 @@
     out_ref, *refs,
 ):
     if fused:
-        second_ref, bias_s = refs
+        second_ref, bias_s, inv_s, e_s, gated_s, new_s = refs
     else:
-        (bias_s,) = refs
+        bias_s, inv_s, e_s, gated_s = refs
     peers = recv_ref.shape[0]
     rows, n, chan = x_s.shape
     tiles = n // LANES
@@ -187,7 +190,7 @@
     for s in range(peers):
         at = slice(s * rows, (s + 1) * rows)
         for block, owner in ((recv_ref[s, base:], core), (other_ref[s], 1 - core)):
-            extra = block.astype(F32)
+            extra = block.astype(F32) * LOG2E
             for t in range(tiles):
                 cs = slice(t * LANES, (t + 1) * LANES)
                 for h in range(half):
@@ -195,57 +198,57 @@
                     head = owner * half + h
                     bias_s[head, at, cs] = extra[start : start + rows] + term_ref[head, at, cs]
 
-    scaling = dim ** (-0.5)
+    scaling = dim ** (-0.5) * LOG2E
     w_out = wo_ref[...]
-    w_dist = wd_ref[...]
-    d_bias = db_ref[:, :1]
-
-    def score(j, t):
-        return dot_nn(k_s[j], spread_s[j, t])
-
-    def attend(j, t, scores):
+
+    def soften(j, t):
         cs = slice(t * LANES, (t + 1) * LANES)
-        gated = []
+        scores = dot_nn(k_s[j], spread_s[j, t])
+        for h in range(heads):
+            s = scores[:, h * LANES : (h + 1) * LANES] * scaling + bias_s[h, :, cs]
+            e = jnp.exp2(s - jnp.max(s, 0, keepdims=True))
+            inv_s[j, t, h : h + 1] = 1.0 / jnp.sum(e, 0, keepdims=True)
+            e_s[j, t, :, h * LANES : (h + 1) * LANES] = e.astype(BF16)
+
+    def combine(j, t):
+        cs = slice(t * LANES, (t + 1) * LANES)
         for first in range(0, heads, 2):
-            weights, scales = [], []
-            for h in (first, first + 1):
-                s = scores[:, h * LANES : (h + 1) * LANES] * scaling + bias_s[h, :, cs]
-                e = jnp.exp(s - jnp.max(s, 0, keepdims=True))
-                scales.append(1.0 / jnp.sum(e, 0, keepdims=True))
-                weights.append(e.astype(BF16))
-            o = dot_nn(v_s[j, first * dim : (first + 2) * dim, :], jnp.concatenate(weights, 1))
+            o = dot_nn(v_s[j, first * dim : (first + 2) * dim], e_s[j, t, :, first * LANES : (first + 2) * LANES])
             for side in range(2):
                 h = first + side
                 part = o[side * dim : (side + 1) * dim, side * LANES : (side + 1) * LANES]
-                gated.append((g_s[j, h * dim : (h + 1) * dim, cs] * (part * scales[side])).astype(BF16))
-        return dot_tn(jnp.concatenate(gated, 0), w_out).astype(BF16)
-
-    def residual(j, update):
-        new = (x_s[j].astype(F32) + update.astype(F32)).astype(BF16)
-        second_ref[j] = (dot_nt(w_dist, new) + d_bias).astype(BF16)
-        return new.astype(F32).reshape(peers, rows, chan)
+                mine = slice(h * dim, (h + 1) * dim)
+                gated_s[j, mine, cs] = (g_s[j, mine, cs] * (part * inv_s[j, t, h : h + 1])).astype(BF16)
 
     if not fused:
 
         @pl.loop(0, rows)
         def _(j):
             for t in range(tiles):
-                out_ref[j, t * LANES : (t + 1) * LANES] = attend(j, t, score(j, t))
+                soften(j, t)
+                combine(j, t)
+            out_ref[j] = dot_tn(gated_s[j], w_out).astype(BF16)
 
         return
 
-    both = []
-    scores = score(0, 0)
+    for stage in (soften, combine):
+        for j in range(rows):
+            for t in range(tiles):
+                stage(j, t)
     for j in range(rows):
-        later = score(j + 1, 0) if j + 1 < rows and tiles == 1 else None
-        updates = [attend(j, 0, scores)]
-        for t in range(1, tiles):
-            updates.append(attend(j, t, score(j, t)))
-        both.append(residual(j, jnp.concatenate(updates, 0)))
-        scores = later if tiles == 1 or j + 1 == rows else score(j + 1, 0)
-        if j % 2:
-            out_ref[:, (j - 1) * rows : (j + 1) * rows, :] = jnp.concatenate(both, 1).astype(BF16)
-            both = []
+        update = dot_tn(gated_s[j], w_out).astype(BF16)
+        new_s[j] = (x_s[j].astype(F32) + update.astype(F32)).astype(BF16)
+    for j in range(0, rows, 2):
+        both = [new_s[j + side].astype(F32).reshape(peers, rows, chan) for side in range(2)]
+        out_ref[:, j * rows : (j + 2) * rows, :] = jnp.concatenate(both, 1).astype(BF16)
+    logits_of(new_s, wd_ref[...], db_ref[:, :1], second_ref)
+
+
+def logits_of(new_ref, w_dist, d_bias, out_ref):
+    rows, n, chan = new_ref.shape
+    logits = dot_nt(w_dist, new_ref[...].reshape(rows * n, chan)) + d_bias
+    for j in range(rows):
+        out_ref[j] = logits[:, j * n : (j + 1) * n].astype(BF16)
 
 
 def finish_kernel(recv_ref, mirror_ref, wd_ref, db_ref, new_hbm, dist_hbm, new_ref, dist_ref, sems):
@@ -259,11 +262,9 @@
         new_ref[:, at, :] = dot_nn(swap, both).astype(BF16).reshape(rows, group, chan)
     copies = [pltpu.make_async_copy(new_ref, new_hbm, sems.at[0])]
     copies[0].start()
-    w_dist = wd_ref[...]
-    d_bias = db_ref[:, :1]
+    logits_of(new_ref, wd_ref[...], db_ref[:, :1], dist_ref)
     for i in range(rows):
-        logits = (dot_nt(w_dist, new_ref[i]) + d_bias).astype(BF16)
-        dist_ref[i] = (logits.astype(F32) + mirror_ref[i].astype(F32)).astype(BF16)
+        dist_ref[i] = (dist_ref[i].astype(F32) + mirror_ref[i].astype(F32)).astype(BF16)
         if i % 2:
             at = pl.ds(i - 1, 2)
             copies.append(pltpu.make_async_copy(dist_ref.at[at], dist_hbm.at[at], sems.at[1 + i // 2]))
@@ -315,6 +316,7 @@
             pltpu.VMEM(pair_act.shape, BF16),
             pltpu.VMEM(gain.shape, F32),
             pltpu.VMEM((heads, chan), BF16),
+            pltpu.VMEM(pair_act.shape, BF16),
             pltpu.VMEM((peers, length, chan), BF16),
             pltpu.SemaphoreType.DMA((rows + 2,)),
             pltpu.SemaphoreType.DMA((2,)),
@@ -360,7 +362,13 @@
         functools.partial(attend_kernel, heads, fused),
         outs,
         [received, other_bias, term, w_out, wd_t, db_col, x_cols, spread, keys, values, gates],
-        scratch=[pltpu.VMEM((heads, n, n), F32)],
+        scratch=[
+            pltpu.VMEM((heads, n, n), F32),
+            pltpu.VMEM((rows, tiles, heads, LANES), F32),
+            pltpu.VMEM((rows, tiles, n, heads * LANES), BF16),
+            pltpu.VMEM((rows, width, n), BF16),
+        ]
+        + [pltpu.VMEM((rows, n, chan), BF16)] * fused,
     )
     if fused:
         to_rows, mirror = result

time: 40.3 us -> 39 us (0.968)
  Pallas kernels: 8.07 us -> 6.77 us
    pallas_call x5, Pallas kernels: 8.07 us -> 6.77 us  [call(): pl.pallas_call(kernel, out_shape=[jax.ShapeDtypeStruct(s, d) for s, d in...]
where the time goes in v2:
time: 39 us; the launch traced here: 38.7 us
  blocking collectives  13.2 us (34%)
  waiting for transfers between devices  9.64 us (25%)
  starting transfers between devices  7.63 us (20%)
  Pallas kernels  6.77 us (17%)
  between operations  0.77 us (2%)
  local copies, waits for them, and re-layouts  0.66 us (2%)
    all_to_all x1, blocking collectives, all_to_all(): lax.all_to_all(blocks, 'row', split_axis=0, concat_axis=0, tiled=True)  13.2 us
    all_to_all x1, waiting for transfers between devices, all_to_all(): lax.all_to_all(blocks, 'row', split_axis=0, concat_axis=0, tiled=True)  9.57 us
    all_to_all x1, starting transfers between devices, all_to_all(): lax.all_to_all(blocks, 'row', split_axis=0, concat_axis=0, tiled=True)  7.52 us
    pallas_call x5, Pallas kernels, call(): pl.pallas_call(kernel, out_shape=[jax.ShapeDtypeStruct(s, d) for s, d in...  6.77 us
  transfers between devices with their start and end apart: 2, of which 2 were waited for; matrix products, arithmetic and copies ran while one was open for 0% of the time, Pallas kernels for 5%

profile of v2, /device:TPU:0, one launch (start us, length us, event | category | flops | bytes accessed | tf_op | source)
XLA Modules:
  0.0 38.7 jit_solution(11742759974081831534)
XLA Ops:
  0.6 2.2 %shard_map.113 = bf16[16,80,128]{2,1,0:T(8,128)(2,1)} custom-call(bf16[8,128,128]{2,1,0:T(8,128)(2,1)} %x_hbm.1, f32[1,128]{1,0:T(1,128)} %bitcast.10, bf16[4,128]{1,0:T(4,128)(2,1)} %bitcast.15), custom_call_target="tpu_custom_call" | custom-call | tf_op jit(solution)/shard_map/pallas_call | solution.py:278
  2.9 0.0 copy-start
  2.9 0.0 copy-start.1
  2.9 0.0 copy-start.2
  2.9 0.0 copy-start.5
  2.9 0.0 copy-start.6
  2.9 0.0 copy-start.7
  2.9 7.5 %all-to-all-start = ((bf16[16,80,128]{2,1,0:T(8,128)(2,1)}), bf16[16,80,128]{2,1,0:T(8,128)(2,1)S(1)}, u32[]{:S(2)}, u32[]{:S(2)}) async-start(bf16[16,80,128]{2,1,0:T(8,128)(2,1)} %shard_map.113), calls=%async_computation | async-start | bytes 655360 | tf_op jit(solution)/shard_map/all_to_all | solution.py:294
  10.5 0.0 copy-start.3
  10.5 0.0 copy-start.4
  10.5 0.0 copy-done
  10.5 0.0 copy-done.1
  10.5 0.0 copy-done.2
  10.5 0.0 copy-done.5
  10.6 0.6 %copy-done.3 = f32[128]{0:T(128)S(1)} copy-done((f32[128]{0:T(128)S(1)}, f32[128]{0:T(128)}, u32[]{:S(2)}) %copy-start.3) | copy-done | bytes 536
  11.1 0.0 copy-done.4
  11.2 0.8 %shard_map.114 = (f32[4,128,128]{2,1,0:T(8,128)S(1)}, bf16[512,128]{1,0:T(8,128)(2,1)S(1)}, f32[64,128]{1,0:T(8,128)S(1)}, f32[1,128]{1,0:T(1,128)S(1)}, bf16[12...) custom-call(s32[1,128]{1,0:T(1,128)S(1)} %bitcast.12, s32[1,128]{1,0:T(1,128)S(1)} %bitcast.13, f32[2,4]{1,0:T(2,128)S(1)} %copy-done.4, ...), custom_call_target="tpu_custom_call" | custom-call | tf_op jit(solution)/shard_map/pallas_call | solution.py:278
  12.0 9.6 %all-to-all-done.recv_ref = bf16[16,80,128]{2,1,0:T(8,128)(2,1)S(1)} async-done(((bf16[16,80,128]{2,1,0:T(8,128)(2,1)}), bf16[16,80,128]{2,1,0:T(8,128)(2,1)S(1)}, u32[]{:S(2)}, u32[]{:S(2)}) %all-to-all-start) | async-done | bytes 327712 | tf_op jit(solution)/shard_map/all_to_all | solution.py:294
  21.6 0.1 collective-permute-start
  21.7 1.1 %shard_map.115 = (bf16[8,128,128]{2,1,0:T(8,128)(2,1)S(1)}, bf16[8,1,128,512]{3,2,1,0:T(8,128)(2,1)S(1)}, bf16[8,128,128]{2,1,0:T(8,128)(2,1)S(1)}, bf16[8,128,128]{2,1,0:T(8,128)(2,1)S(1)}, f32[8,128,128]{2,1,0:T(8,128)S(1)}) custom-call(bf16[16,80,128]{2,1,0:T(8,128)(2,1)S(1)} %all-to-all-done.recv_ref, f32[1,128]{1,0:T(1,128)S(1)} %get-tuple-element.35.gain_ref, ...), custom_call_target="tpu_custom_call" | custom-call | tf_op jit(solution)/shard_map/pallas_call | solution.py:278
  22.8 0.1 collective-permute-done.other_ref
  22.8 1.5 %shard_map.116 = (bf16[16,64,128]{2,1,0:T(8,128)(2,1)S(1)}, bf16[8,64,128]{2,1,0:T(8,128)(2,1)S(1)}) custom-call(bf16[16,80,128]{2,1,0:T(8,128)(2,1)S(1)} %all-to-all-done.recv_ref, bf16[16,16,128]{2,1,0:T(8,128)(2,1)S(1)} %collective-permute-done.other_ref, f32[4,128,128]{2,1,0:T(8,128)S(1)} %get-tuple-element.31.term_ref, ...), custom_call_target="tpu_custom_call" | custom-call | tf_op jit(solution)/shard_map/pallas_call | solution.py:278
  24.4 13.2 %all_to_all.10.recv_ref = bf16[16,64,128]{2,1,0:T(8,128)(2,1)S(1)} all-to-all(bf16[16,64,128]{2,1,0:T(8,128)(2,1)S(1)} %get-tuple-element.42), channel_id=1, replica_groups=mesh['dp'=2,'head'=1,'row'=16] {'row'}, dimensions={0} | all-to-all | bytes 524288 | tf_op jit(solution)/shard_map/all_to_all | solution.py:294
  37.6 1.1 %shard_map.117 = (bf16[8,128,128]{2,1,0:T(8,128)(2,1)}, bf16[8,64,128]{2,1,0:T(8,128)(2,1)}) custom-call(bf16[16,64,128]{2,1,0:T(8,128)(2,1)S(1)} %all_to_all.10.recv_ref, bf16[8,64,128]{2,1,0:T(8,128)(2,1)S(1)} %get-tuple-element.43.mirror_ref, bf16[64,128]{1,0:T(8,128)(2,1)S(1)} %get-tuple-element.33.wd_ref, f32[64,128]{1,0:T(8,128)S(1)} %get-tuple-element.34.db_ref), custom_call_target="tpu_custom_call" | custom-call | tf_op jit(solution)/shard_map/pallas_call | solution.py:278
  (3 shorter events, 0.0 us)
Async XLA Ops:
  2.9 7.6 %copy-start = (bf16[128,4,128]{2,1,0:T(4,128)(2,1)S(1)}, bf16[128,4,128]{2,1,0:T(4,128)(2,1)}, u32[]{:S(2)}) copy-start(bf16[128,4,128]{2,1,0:T(4,128)(2,1)} %w_ref.1) | copy-start | bytes 393220
  2.9 7.6 %copy-start.1 = (bf16[4,32,128]{2,1,0:T(8,128)(2,1)S(1)}, bf16[4,32,128]{2,1,0:T(8,128)(2,1)}, u32[]{:S(2)}) copy-start(bf16[4,32,128]{2,1,0:T(8,128)(2,1)} %param.17) | copy-start | bytes 98308
  2.9 7.6 %copy-start.2 = (bf16[128,64]{0,1:T(8,128)(2,1)S(1)}, bf16[128,64]{0,1:T(8,128)(2,1)}, u32[]{:S(2)}) copy-start(bf16[128,64]{0,1:T(8,128)(2,1)} %param.18) | copy-start | bytes 49156
  2.9 7.6 %copy-start.5 = (s32[128]{0:T(128)S(1)}, s32[128]{0:T(128)}, u32[]{:S(2)}) copy-start(s32[128]{0:T(128)} %param.11) | copy-start | bytes 1540
  2.9 7.6 %copy-start.6 = (s32[128]{0:T(128)S(1)}, s32[128]{0:T(128)}, u32[]{:S(2)}) copy-start(s32[128]{0:T(128)} %param.12) | copy-start | bytes 1540
  2.9 7.6 %copy-start.7 = (f32[64]{0:T(128)S(1)}, f32[64]{0:T(128)}, u32[]{:S(2)}) copy-start(f32[64]{0:T(128)} %param.19) | copy-start | bytes 772
  2.9 18.6 %all-to-all-start = ((bf16[16,80,128]{2,1,0:T(8,128)(2,1)}), bf16[16,80,128]{2,1,0:T(8,128)(2,1)S(1)}, u32[]{:S(2)}, u32[]{:S(2)}) async-start(bf16[16,80,128]{2,1,0:T(8,128)(2,1)} %shard_map.113), calls=%async_computation | async-start | bytes 655360 | tf_op jit(solution)/shard_map/all_to_all | solution.py:294
  10.5 0.7 %copy-start.3 = (f32[128]{0:T(128)S(1)}, f32[128]{0:T(128)}, u32[]{:S(2)}) copy-start(f32[128]{0:T(128)} %param.13) | copy-start | bytes 1540
  10.5 0.7 %copy-start.4 = (f32[2,4]{1,0:T(2,128)S(1)}, f32[2,4]{1,0:T(2,128)}, u32[]{:S(2)}) copy-start(f32[2,4]{1,0:T(2,128)} %cb_ref.1) | copy-start | bytes 100
  21.6 1.3 %collective-permute-start = (bf16[16,16,128]{2,1,0:T(8,128)(2,1)S(1)}, bf16[16,16,128]{2,1,0:T(8,128)(2,1)S(1)}, u32[]{:S(2)}, u32[]{:S(2)}) collective-permute-start(bf16[16,16,128]{2,1,0:T(8,128)(2,1)S(1)} %slice.3), channel_id=1, source_target_pairs={{0,1},{1,0},{2,3},{3,2},{4,5},{5,4},{6,7},{7,6},{8,9},{9,8},{10,11... | collective-permute-start | bytes 196616 | tf_op jit(solution)/shard_map/ppermute | solution.py:290
